TPU v7x, 256 devices: a whole 4x4x8 slice. The times are simulated.
256 devices in a mesh: grp: 32 (over x, y, z_lo), tp: 8 (over z_hi, core).
Axes of the slice: x: 4, y: 4, z: 8 (z_hi: 4, z_lo: 2; z = z_hi * 2 + z_lo), core: 2. Of those that a mesh axis runs over, the one named last changes fastest.
Arguments:
- queries: bfloat16 [8192, 4096], P('grp', 'tp'), may hold values from -24 to 24
- suffix_kv: bfloat16 [8192, 2, 1024], P('grp', None, 'tp'), may hold values from -12 to 12
- prefix_cache: bfloat16 [32, 2, 1536, 1024], P('grp', None, None, 'tp'), may hold values from -20 to 20
- out_weight: bfloat16 [4096, 8192], P('tp'), may hold values from -0.5 to 0.5
- readers: int32 [32, 16], P('grp'), may hold values from 0 to 31, all different within a row
- owner: int32 [32], replicated, may hold values from 0 to 31, each once
- lengths: int32 [32, 16], P('grp'), may hold values from 1 to 20, 256 in all within a row
Outputs:
- mixed: bfloat16 [8192, 8192], P('grp', 'tp')
Inputs may be any that keep to these rules, and one draw needn't show every extreme that they name: The 16 prefixes of one row of readers are different; every prefix is read by some device. `owner`: each grp device holds exactly one prefix. `lengths`: each row sums to 256 and its largest entry is 20.
All inputs are finite; a program needn't handle non-finite values.
Results may differ from a plain program's by a relative error of at most 0.025.
Values may be sent and summed in bfloat16 or wider, within the bound.
A program may use at most 128 MiB of HBM per device.

v0:
```python
import jax
import jax.numpy as jnp
from jax import lax
from jax.sharding import PartitionSpec as P

HEAD = 128
MOST = 20


NEG_FILL = -1e30


def attend(queries_in, own_keys, own_values, visible):
    inv_root = queries_in.shape[-1] ** (-0.5)
    scores = (
        jnp.einsum("rkge,pke->rkgp", queries_in, own_keys, preferred_element_type=jnp.float32)
        * inv_root
    )
    if visible is not None:
        scores = jnp.where(visible[:, None, None, :], scores, NEG_FILL)
    row_top = jnp.max(scores, axis=3)
    weights = jnp.exp(scores - row_top[..., None])
    row_total = jnp.sum(weights, axis=3)
    weighted = jnp.einsum(
        "rkgp,pke->rkge",
        weights.astype(jnp.bfloat16),
        own_values,
        preferred_element_type=jnp.float32,
    )
    return (row_top, row_total, weighted)


def combine(first_part, second_part):
    joint_top = jnp.maximum(first_part[0], second_part[0])
    first_factor = jnp.exp(first_part[0] - joint_top)
    second_factor = jnp.exp(second_part[0] - joint_top)
    joint_total = first_part[1] * first_factor + second_part[1] * second_factor
    joint_weighted = (
        first_part[2] * first_factor[..., None] + second_part[2] * second_factor[..., None]
    )
    return (joint_top, joint_total, joint_weighted)


def local(queries, suffix_kv, prefix_cache, out_weight, readers, owner, lengths):
    row_count = queries.shape[0]
    row_width = queries.shape[1]
    kv_local = suffix_kv.shape[2] // HEAD
    per_group = row_width // (kv_local * HEAD)
    holders_count = owner.shape[0]
    seq_count = readers.shape[1]
    grouped = queries.reshape(row_count, kv_local, per_group, HEAD)
    seq_lens = lengths[0]
    seq_ends = jnp.cumsum(seq_lens)
    seq_starts = seq_ends - seq_lens
    row_index = jnp.arange(row_count, dtype=jnp.int32)
    seq_of = jnp.sum((row_index[:, None] >= seq_ends[None, :]).astype(jnp.int32), axis=1)
    same_sequence = (seq_of[:, None] == seq_of[None, :]) & (
        row_index[None, :] <= row_index[:, None]
    )
    suffix_keys = suffix_kv[:, 0].reshape(row_count, kv_local, HEAD)
    suffix_values = suffix_kv[:, 1].reshape(row_count, kv_local, HEAD)
    local_part = attend(grouped, suffix_keys, suffix_values, same_sequence)
    padded = jnp.concatenate(
        [grouped, jnp.zeros((MOST, kv_local, per_group, HEAD), jnp.bfloat16)], axis=0
    )
    seq_rows = jax.vmap(lambda first_row: lax.dynamic_slice_in_dim(padded, first_row, MOST, 0))(
        seq_starts
    )
    row_live = jnp.arange(MOST, dtype=jnp.int32)[None, :] < seq_lens[:, None]
    seq_rows = jnp.where(row_live[:, :, None, None, None], seq_rows, jnp.zeros((), jnp.bfloat16))
    device_ids = jnp.arange(holders_count, dtype=jnp.int32)
    holder = jnp.sum(
        jnp.where(readers[0][:, None] == device_ids[None, :], owner[None, :], 0), axis=1
    )
    empty_top = jnp.full((seq_count, MOST, kv_local, per_group), NEG_FILL, jnp.float32)
    empty_total = jnp.zeros((seq_count, MOST, kv_local, per_group), jnp.float32)
    empty_weighted = jnp.zeros((seq_count, MOST, kv_local, per_group, HEAD), jnp.float32)
    block_piece = lax.all_gather(prefix_cache, "grp", axis=0, tiled=True)

    def one_holder(offset, carried):
        holder_block = lax.dynamic_index_in_dim(block_piece, offset, 0, keepdims=False)
        block_keys = holder_block[0].reshape(-1, kv_local, HEAD)
        block_values = holder_block[1].reshape(-1, kv_local, HEAD)
        is_holder = holder == offset
        chosen = jnp.sum(
            jnp.where(is_holder[:, None, None, None, None], seq_rows, jnp.zeros((), jnp.bfloat16)),
            axis=0,
        )
        computed = attend(chosen, block_keys, block_values, None)
        selector = is_holder[:, None, None, None]
        return (
            jnp.where(selector, computed[0][None], carried[0]),
            jnp.where(selector, computed[1][None], carried[1]),
            jnp.where(selector[..., None], computed[2][None], carried[2]),
        )

    prefix_part = lax.fori_loop(
        0, block_piece.shape[0], one_holder, (empty_top, empty_total, empty_weighted)
    )
    seq_ids = jnp.arange(seq_count, dtype=jnp.int32)
    start_of_row = jnp.sum(
        jnp.where(seq_of[:, None] == seq_ids[None, :], seq_starts[None, :], 0), axis=1
    )
    gather_rows = seq_of * MOST + row_index - start_of_row
    row_parts = tuple(
        (
            jnp.take(member.reshape((seq_count * MOST,) + member.shape[2:]), gather_rows, axis=0)
            for member in prefix_part
        )
    )
    merged = combine(row_parts, local_part)
    attention = (
        (merged[2] / merged[1][..., None]).astype(jnp.bfloat16).reshape(row_count, row_width)
    )
    partial_terms = jnp.dot(attention, out_weight, preferred_element_type=jnp.float32)
    return lax.psum_scatter(
        partial_terms.astype(jnp.bfloat16), "tp", scatter_dimension=1, tiled=True
    )


def solution(mesh):
    return jax.shard_map(
        local,
        mesh=mesh,
        in_specs=(
            P("grp", "tp"),
            P("grp", None, "tp"),
            P("grp", None, None, "tp"),
            P("tp", None),
            P("grp", None),
            P(),
            P("grp", None),
        ),
        out_specs=P("grp", "tp"),
        check_vma=False,
    )
```

profile of v0, /device:TPU:1, one launch (start us, length us, event | category | flops | bytes accessed | tf_op | source)
XLA Modules:
  0.0 745.2 jit_solution(12794672067022793669)
XLA Ops:
  16.4 535.9 %all-gather.2.cloned.1.call-done = bf16[32,2,1536,128]{3,2,1,0:T(8,128)(2,1)} async-done(((bf16[1,2,1536,128]{3,2,1,0:T(8,128)(2,1)}), bf16[32,2,1536,128]{3,2,1,0:T(8,128)(2,1)}) %all-gather.2.cloned.1.call-update) | async-done | bytes 25165840 | tf_op jit(solution)/shard_map/all_gather | solution.py:78
  552.3 118.2 %while.20 = (s32[]{:T(128)}, f32[16,20,1,4]{1,3,2,0:T(4,128)S(1)}, f32[16,20,1,4]{1,3,2,0:T(4,128)S(1)}, f32[16,20,1,4,128]{4,3,2,1,0:T(4,128)S(1)}, s32[16]{0:T...) while((s32[]{:T(128)}, f32[16,20,1,4]{1,3,2,0:T(4,128)S(1)}, ...), condition=%wide.region_8.9_spmd.clone, body=%wide.region_4.8_spmd.clone.sunk | while | flops 64301936 | bytes 4126868 | solution.py:97
  552.6 1.5 fusion.48
  556.3 1.5 fusion.48
  560.0 1.5 fusion.48
  563.7 1.5 fusion.48
  567.3 1.5 fusion.48
  571.0 1.5 fusion.48
  574.7 1.5 fusion.48
  578.4 1.5 fusion.48
  582.1 1.5 fusion.48
  585.8 1.5 fusion.48
  589.5 1.5 fusion.48
  593.2 1.5 fusion.48
  596.9 1.5 fusion.48
  600.6 1.5 fusion.48
  604.3 1.5 fusion.48
  608.0 1.5 fusion.48
  611.7 1.5 fusion.48
  619.1 1.5 fusion.48
  622.8 1.5 fusion.48
  630.1 1.5 fusion.48
  633.8 1.5 fusion.48
  641.2 1.5 fusion.48
  644.9 1.5 fusion.48
  652.3 1.5 fusion.48
  656.0 1.5 fusion.48
  659.7 1.5 fusion.48
  663.4 1.5 fusion.48
  667.1 1.5 fusion.48
  674.4 7.7 %convolution_convert_fusion = bf16[256,8192]{1,0:T(8,128)(2,1)} fusion(bf16[256,512]{0,1:T(8,128)(2,1)S(1)} %bitcast.167, bf16[512,8192]{1,0:T(8,128)(2,1)} %param.14), kind=kOutput, calls=%fused_computation.22 | convolution fusion | flops 2149580800 | bytes 12845056 | tf_op jit(solution)/shard_map/dot_general | solution.py:115
  682.1 56.2 %reduce-scatter.2.cloned.1.call-done = bf16[256,1024]{1,0:T(8,128)(2,1)} async-done(((bf16[256,8192]{1,0:T(8,128)(2,1)}), bf16[256,1024]{1,0:T(8,128)(2,1)}) %reduce-scatter.2.cloned.1.call-update) | async-done | bytes 524304 | tf_op jit(solution)/shard_map/reduce_scatter | solution.py:116
  (274 shorter events, 89.3 us)
Async XLA Ops:
  6.5 545.8 %all-gather.2.cloned.1.call-start = ((), (), s32[]{:S(2)}) async-start(), calls=%async_computation.1 | async-start | bytes 25952256 | tf_op jit(solution)/shard_map/all_gather | solution.py:78
  7.3 731.1 %reduce-scatter.2.cloned.1.call-start = ((), (), s32[]{:S(2)}) async-start(), calls=%async_computation.2 | async-start | bytes 4718592 | tf_op jit(solution)/shard_map/reduce_scatter | solution.py:116
Sparse Core Ops, SparseCore 0:
  9.1 543.1 all-gather.1
  682.3 56.0 reduce-scatter.1
where the time goes:
time: 750 us; the launch traced here: 745 us
  waiting for transfers between devices  593 us (79%)
  matrix products  97.7 us (13%)
  other arithmetic  31.3 us (4%)
  between operations  13.6 us (2%)
  local copies, waits for them, and re-layouts  8.08 us (1%)
    all_gather x1, waiting for transfers between devices, local(): block_piece = lax.all_gather(prefix_cache, 'grp', axis=0, tiled=True)  536 us
    reduce_scatter x1, waiting for transfers between devices, local(): lax.psum_scatter(partial_terms.astype(jnp.bfloat16), 'tp', scatter_dimens...  56.2 us
    dot_general x33, matrix products, attend(): jnp.einsum('rkge,pke->rkgp', queries_in, own_keys, preferred_element_type...  47.9 us
    dot_general x33, matrix products, attend(): jnp.einsum('rkgp,pke->rkge', weights.astype(jnp.bfloat16), own_values, pr...  42.1 us
  transfers between devices with their start and end apart: 2, of which 2 were waited for; matrix products, arithmetic and copies ran while one was open for 1% of the time, Pallas kernels for 0%

commit v1 on v0

v1 whole, which is shorter than its diff:
```python
import math

import jax
import jax.numpy as jnp
from jax import lax
from jax.experimental import pallas as pl
from jax.experimental.pallas import tpu as pltpu
from jax.sharding import PartitionSpec as P

HEAD = 128
MOST = 20
MAIN = 16
TAIL = MOST - MAIN
PER = 4
SLOT = MOST * PER
NX, NY, NZ = 4, 4, 2
HOLDERS = NX * NY * NZ
GROUP = 8
NEG = -1e30
FACTOR = math.log2(math.e) / math.sqrt(HEAD)
F32 = jnp.float32
BF16 = jnp.bfloat16


def dot(a, b):
    return jnp.dot(a, b, preferred_element_type=F32)


def dot_t(a, b):
    return lax.dot_general(a, b, (((1,), (1,)), ((), ())), preferred_element_type=F32)


def shifted(x, y, z, d, sign):
    dx, dy, dz = d // (NY * NZ), (d // NZ) % NY, d % NZ
    if sign > 0:
        nx, ny, nz = (x + dx) % NX, (y + dy) % NY, (z + dz) % NZ
    else:
        nx, ny, nz = (x + NX - dx) % NX, (y + NY - dy) % NY, (z + NZ - dz) % NZ
    return nx * (NY * NZ) + ny * NZ + nz


def row_places(shape, axis, me, readers, owner, lengths):
    x, y, z = me
    rows = lax.broadcasted_iota(jnp.int32, shape, axis)
    slot = jnp.zeros(shape, jnp.int32)
    first = jnp.zeros(shape, jnp.int32)
    start = jnp.int32(0)
    for s in range(readers.shape[1]):
        holder = owner[readers[0, s]]
        hx, hy, hz = holder // (NY * NZ), (holder // NZ) % NY, holder % NZ
        d = ((hx + NX - x) % NX) * (NY * NZ) + ((hy + NY - y) % NY) * NZ + (hz + NZ - z) % NZ
        inside = rows >= start
        slot = jnp.where(inside, d, slot)
        first = jnp.where(inside, start, first)
        start = start + lengths[0, s]
    return rows, slot, rows - first, first


def one_hot(cond):
    return jnp.where(cond, 1.0, 0.0).astype(BF16)


def attend_kernel(
    q, kv, cache, readers, owner, lengths, out,
    send, recv, back, ret, lback, lret, sufw, suft,
    send_sem, recv_sem, back_sem, ret_sem, lback_sem, lret_sem,
):
    me = lax.axis_index("grp")
    x, y, z = me // (NY * NZ), (me // NZ) % NY, me % NZ
    rows_n = q.shape[0]

    barrier = pltpu.get_barrier_semaphore()

    def greet(d, carry):
        pl.semaphore_signal(
            barrier, inc=1, device_id={"grp": shifted(x, y, z, d, 1)},
            device_id_type=pl.DeviceIdType.MESH,
        )
        return carry

    lax.fori_loop(1, HOLDERS, greet, 0)

    _, slot, place, _ = row_places((1, rows_n), 1, (x, y, z), readers, owner, lengths)
    wide = lax.broadcasted_iota(jnp.int32, (HOLDERS * MAIN, rows_n), 0)
    main_at = jnp.where(place < MAIN, slot * MAIN + place, -1)
    main = dot(one_hot(wide == main_at), q[...]).astype(BF16)
    tail = jnp.zeros((HOLDERS * MAIN, HEAD), F32)
    for k in range(PER):
        cols = slice(k * HEAD, (k + 1) * HEAD)
        send[:, k * MAIN:(k + 1) * MAIN, :] = main[:, cols].reshape(HOLDERS, MAIN, HEAD)
        tail_at = jnp.where(place >= MAIN, slot * MAIN + TAIL * k + place - MAIN, -1)
        tail = tail + dot(one_hot(wide == tail_at), q[:, cols])
    send[:, PER * MAIN:, :] = tail.astype(BF16).reshape(HOLDERS, MAIN, HEAD)

    pl.semaphore_wait(barrier, HOLDERS - 1)

    def dispatch(d):
        return pltpu.make_async_remote_copy(
            src_ref=send.at[d], dst_ref=recv.at[d],
            send_sem=send_sem.at[d], recv_sem=recv_sem.at[d],
            device_id={"grp": shifted(x, y, z, d, 1)},
            device_id_type=pl.DeviceIdType.MESH,
        )

    def give(d):
        return pltpu.make_async_remote_copy(
            src_ref=back.at[d], dst_ref=ret.at[d],
            send_sem=back_sem.at[d], recv_sem=ret_sem.at[d],
            device_id={"grp": shifted(x, y, z, d, -1)},
            device_id_type=pl.DeviceIdType.MESH,
        )

    def give_l(d):
        return pltpu.make_async_remote_copy(
            src_ref=lback.at[d], dst_ref=lret.at[d],
            send_sem=lback_sem.at[d], recv_sem=lret_sem.at[d],
            device_id={"grp": shifted(x, y, z, d, -1)},
            device_id_type=pl.DeviceIdType.MESH,
        )

    def start_dispatch(d, carry):
        dispatch(d).start()
        return carry

    lax.fori_loop(1, HOLDERS, start_dispatch, 0)
    recv[0] = send[0]

    at, slot, place, first = row_places((rows_n, 1), 0, (x, y, z), readers, owner, lengths)
    other = lax.broadcasted_iota(jnp.int32, (rows_n, rows_n), 1)
    visible = (other >= first) & (other <= at)
    keys, values = kv[:, 0, :], kv[:, 1, :]
    for k in range(PER):
        s = dot_t(q[:, k * HEAD:(k + 1) * HEAD], keys)
        s = jnp.where(visible, s, NEG)
        top = jnp.max(s, axis=1, keepdims=True)
        w = jnp.exp2((s - top) * FACTOR)
        total = jnp.sum(w, axis=1, keepdims=True)
        sufw[k] = dot(w.astype(BF16), values)
        suft[k, :, 0:1] = top * FACTOR
        suft[k, :, 1:2] = total

    prefix_keys = cache[0, 0]
    prefix_values = jnp.concatenate(
        [cache[0, 1], jnp.ones((cache.shape[2], HEAD), BF16)], axis=1
    )
    lane = lax.broadcasted_iota(jnp.int32, (SLOT, HEAD), 1)
    sub = lax.broadcasted_iota(jnp.int32, (SLOT, HEAD), 0)
    for a in range(HOLDERS // GROUP):
        low = a * GROUP

        def wait_slot(d, carry):
            dispatch(d).wait_recv()
            return carry

        lax.fori_loop(max(low, 1), low + GROUP, wait_slot, 0)
        block = recv[low:low + GROUP].reshape(GROUP * SLOT, HEAD)
        s = dot_t(block, prefix_keys)
        top = jnp.max(s, axis=1, keepdims=True)
        w = jnp.exp2((s - top) * FACTOR)
        o = dot(w.astype(BF16), prefix_values)
        total = o[:, HEAD:]
        back[low:low + GROUP] = (o[:, :HEAD] / total).astype(BF16).reshape(GROUP, SLOT, HEAD)
        lse = top * FACTOR + jnp.log2(total)
        for i in range(GROUP):
            part = lse[i * SLOT:(i + 1) * SLOT]
            lback[low + i] = jnp.sum(jnp.where(lane == sub, part, 0.0), axis=0, keepdims=True)

        def start_give(d, carry):
            give(d).start()
            give_l(d).start()
            return carry

        lax.fori_loop(max(low, 1), low + GROUP, start_give, 0)

    ret[0] = back[0]
    lret[0] = lback[0]

    cols = lax.broadcasted_iota(jnp.int32, (rows_n, HOLDERS * MAIN), 1)
    from_main = one_hot(cols == jnp.where(place < MAIN, slot * MAIN + place, -1))
    slots = lax.broadcasted_iota(jnp.int32, (rows_n, HOLDERS), 1)
    from_slot = one_hot(slots == slot)
    lanes = lax.broadcasted_iota(jnp.int32, (rows_n, HEAD), 1)

    def wait_ret(d, carry):
        give(d).wait_recv()
        give_l(d).wait_recv()
        return carry

    lax.fori_loop(1, HOLDERS, wait_ret, 0)

    l_all = lret[...].reshape(HOLDERS, HEAD)
    l_high = l_all.astype(BF16)
    l_rest = l_all - l_high.astype(F32)
    l_mid = l_rest.astype(BF16)
    l_low = (l_rest - l_mid.astype(F32)).astype(BF16)
    l_rows = dot(from_slot, l_high) + dot(from_slot, l_mid) + dot(from_slot, l_low)
    tails = ret[:, PER * MAIN:, :].reshape(HOLDERS * MAIN, HEAD)
    for k in range(PER):
        from_tail = one_hot(
            cols == jnp.where(place >= MAIN, slot * MAIN + TAIL * k + place - MAIN, -1)
        )
        mains = ret[:, k * MAIN:(k + 1) * MAIN, :].reshape(HOLDERS * MAIN, HEAD)
        pre = dot(from_main, mains) + dot(from_tail, tails)
        l_at = jnp.where(place < MAIN, MAIN * k + place, MAIN * PER + TAIL * k + place - MAIN)
        l_pre = jnp.sum(jnp.where(lanes == l_at, l_rows, 0.0), axis=1, keepdims=True)
        l_suf = suft[k, :, 0:1]
        top = jnp.maximum(l_pre, l_suf)
        pre_f, suf_f = jnp.exp2(l_pre - top), jnp.exp2(l_suf - top)
        total = pre_f + suf_f * suft[k, :, 1:2]
        out[:, k * HEAD:(k + 1) * HEAD] = (
            (pre * pre_f + sufw[k] * suf_f) / total
        ).astype(BF16)

    def finish(d, carry):
        dispatch(d).wait_send()
        give(d).wait_send()
        give_l(d).wait_send()
        return carry

    lax.fori_loop(1, HOLDERS, finish, 0)


def attend(queries, suffix_kv, cache, readers, owner, lengths):
    rows_n = queries.shape[0]
    vmem = pl.BlockSpec(memory_space=pltpu.VMEM)
    smem = pl.BlockSpec(memory_space=pltpu.SMEM)
    dma = pltpu.SemaphoreType.DMA((HOLDERS,))
    slots = pltpu.VMEM((HOLDERS, SLOT, HEAD), BF16)
    lses = pltpu.VMEM((HOLDERS, 1, HEAD), F32)
    return pl.pallas_call(
        attend_kernel,
        out_shape=jax.ShapeDtypeStruct(queries.shape, BF16),
        in_specs=[vmem, vmem, vmem, smem, smem, smem],
        out_specs=vmem,
        scratch_shapes=[
            slots, slots, slots, slots, lses, lses,
            pltpu.VMEM((PER, rows_n, HEAD), F32),
            pltpu.VMEM((PER, rows_n, HEAD), F32),
            dma, dma, dma, dma, dma, dma,
        ],
        compiler_params=pltpu.CompilerParams(
            collective_id=0, has_side_effects=True, vmem_limit_bytes=56 * 1024 * 1024
        ),
        cost_estimate=pl.CostEstimate(
            flops=4 * HOLDERS * SLOT * cache.shape[2] * HEAD,
            bytes_accessed=4 * 1024 * 1024,
            transcendentals=HOLDERS * SLOT * cache.shape[2],
        ),
        name="attend",
    )(queries, suffix_kv, cache, readers, owner, lengths)


def local(queries, suffix_kv, prefix_cache, out_weight, readers, owner, lengths):
    attention = attend(queries, suffix_kv, prefix_cache, readers, owner, lengths)
    partial = jnp.dot(attention, out_weight, preferred_element_type=F32)
    return lax.psum_scatter(partial.astype(BF16), "tp", scatter_dimension=1, tiled=True)


def solution(mesh):
    return jax.shard_map(
        local,
        mesh=mesh,
        in_specs=(
            P("grp", "tp"),
            P("grp", None, "tp"),
            P("grp", None, None, "tp"),
            P("tp", None),
            P("grp", None),
            P(),
            P("grp", None),
        ),
        out_specs=P("grp", "tp"),
        check_vma=False,
    )
```

time: 750 us -> 117 us (0.16)
  waiting for transfers between devices: 593 us -> 61.2 us
  matrix products: 97.7 us -> 7.77 us
  Pallas kernels: 0 us -> 33.7 us
  other arithmetic: 31.3 us -> 0 us
  local copies, waits for them, and re-layouts: 8.08 us -> 0 us
    all_gather x1 -> x0, waiting for transfers between devices: 536 us -> none  [local(): block_piece = lax.all_gather(prefix_cache, 'grp', axis=0, tiled=True)]
    dot_general x67 -> x1, matrix products: 97.7 us -> 7.77 us  [local(): partial = jnp.dot(attention, out_weight, preferred_element_type=F32)]
    pallas_call x0 -> x1, Pallas kernels: none -> 33.7 us  [attend(): pl.pallas_call(attend_kernel, out_shape=jax.ShapeDtypeStruct(queries.shap...]
    reduce_sum x68 -> x0, other arithmetic: 16.6 us -> none  [the longest x32 8.07 us: one_holder(): jnp.sum(jnp.where(is_holder[:, None, None, None, None], seq_rows, jnp.zer...]
    select_n x65 -> x0, other arithmetic: 12.3 us -> none  [the longest x32 8.84 us: one_holder(): jnp.where(selector[..., None], computed[2][None], carried[2])]
  transfers between devices with their start and end apart: 2 -> 1, of which waited for: 2 -> 1; matrix products, arithmetic and copies ran while one was open for 1% -> 0% of each run, Pallas kernels for 0% -> 0%
where the time goes in v1:
time: 117 us; the launch traced here: 116 us
  waiting for transfers between devices  61.2 us (52%)
  Pallas kernels  33.7 us (29%)
  between operations  13.4 us (11%)
  matrix products  7.77 us (7%)
    reduce_scatter x1, waiting for transfers between devices, local(): lax.psum_scatter(partial.astype(BF16), 'tp', scatter_dimension=1, tiled=T...  61.2 us
    pallas_call x1, Pallas kernels, attend(): pl.pallas_call(attend_kernel, out_shape=jax.ShapeDtypeStruct(queries.shap...  33.7 us
    dot_general x1, matrix products, local(): partial = jnp.dot(attention, out_weight, preferred_element_type=F32)  7.77 us
  transfers between devices with their start and end apart: 1, of which 1 were waited for; matrix products, arithmetic and copies ran while one was open for 0% of the time, Pallas kernels for 0%

profile of v1, /device:TPU:1, one launch (start us, length us, event | category | flops | bytes accessed | tf_op | source)
XLA Modules:
  0.0 116.1 jit_solution(6705789816249599587)
XLA Ops:
  6.5 0.0 reduce-scatter.2.cloned.1.call-start
  6.5 33.7 %attend.1 = bf16[256,512]{1,0:T(8,128)(2,1)} custom-call(bf16[256,512]{1,0:T(8,128)(2,1)} %q.1, bf16[256,2,128]{2,1,0:T(2,128)(2,1)} %kv.1, bf16[1,2,1536,128]{3,2,1,0:T(8,128)(2,1)} %cache.1, s32[1,16]{1,0:T(1,128)} %readers.1, s32[32]{0:T(128)} %owner.1, s32[1,16]{1,0:T(1,128)} %lengths.1), custom_call_target="tpu_custom_call" | custom-call | flops 2013265920 | bytes 4194304 | tf_op jit(solution)/shard_map/attend/pallas_call | solution.py:230
  40.3 7.8 %convolution_convert_fusion = bf16[256,8192]{1,0:T(8,128)(2,1)} fusion(bf16[256,512]{1,0:T(8,128)(2,1)} %attend.1, bf16[512,8192]{1,0:T(8,128)(2,1)} %param.10), kind=kOutput, calls=%fused_computation | convolution fusion | flops 2149580800 | bytes 12845056 | tf_op jit(solution)/shard_map/dot_general | solution.py:255
  48.0 0.0 reduce-scatter.2.cloned.1.call-update
  48.1 61.2 %reduce-scatter.2.cloned.1.call-done = bf16[256,1024]{1,0:T(8,128)(2,1)} async-done(((bf16[256,8192]{1,0:T(8,128)(2,1)}), bf16[256,1024]{1,0:T(8,128)(2,1)}) %reduce-scatter.2.cloned.1.call-update) | async-done | bytes 524304 | tf_op jit(solution)/shard_map/reduce_scatter | solution.py:256
Async XLA Ops:
  6.5 102.7 %reduce-scatter.2.cloned.1.call-start = ((), (), s32[]{:S(2)}) async-start(), calls=%async_computation.1 | async-start | bytes 4718592 | tf_op jit(solution)/shard_map/reduce_scatter | solution.py:256
Sparse Core Ops, SparseCore 0:
  48.2 61.0 reduce-scatter.1

commit v2 on v1

--- a/solution.py
+++ b/solution.py
@@ -16,6 +16,10 @@
 NX, NY, NZ = 4, 4, 2
 HOLDERS = NX * NY * NZ
 GROUP = 8
+RING = 4
+CORES = 2
+HOPS = RING - 1
+PIECES = 4
 NEG = -1e30
 FACTOR = math.log2(math.e) / math.sqrt(HEAD)
 F32 = jnp.float32
@@ -61,13 +65,20 @@
 
 
 def attend_kernel(
-    q, kv, cache, readers, owner, lengths, out,
+    q, kv, cache, weight, readers, owner, lengths, out,
     send, recv, back, ret, lback, lret, sufw, suft,
+    w_own, w_sib, att, att_sib, part, going, coming,
     send_sem, recv_sem, back_sem, ret_sem, lback_sem, lret_sem,
+    own_sem, sib_send, sib_recv, att_send, att_recv, go_sem, come_sem,
 ):
     me = lax.axis_index("grp")
     x, y, z = me // (NY * NZ), (me // NZ) % NY, me % NZ
+    tp = lax.axis_index("tp")
+    h, core = tp // CORES, tp % CORES
+    sibling = h * CORES + 1 - core
+    beside = [((h + 1) % RING) * CORES + core, ((h + RING - 1) % RING) * CORES + core]
     rows_n = q.shape[0]
+    wide_out = out.shape[1]
 
     barrier = pltpu.get_barrier_semaphore()
 
@@ -79,6 +90,26 @@
         return carry
 
     lax.fori_loop(1, HOLDERS, greet, 0)
+    for partner in [sibling] + beside:
+        pl.semaphore_signal(
+            barrier, inc=1, device_id={"tp": partner}, device_id_type=pl.DeviceIdType.MESH
+        )
+
+    def columns(b, of_core):
+        return pl.ds(pl.multiple_of((b * CORES + of_core) * wide_out, wide_out), wide_out)
+
+    def fetch(b):
+        return pltpu.make_async_copy(weight.at[:, columns(b, core)], w_own.at[b], own_sem.at[b])
+
+    def swap(b):
+        return pltpu.make_async_remote_copy(
+            src_ref=weight.at[:, columns(b, 1 - core)], dst_ref=w_sib.at[b],
+            send_sem=sib_send.at[b], recv_sem=sib_recv.at[b],
+            device_id={"tp": sibling}, device_id_type=pl.DeviceIdType.MESH,
+        )
+
+    for b in range(RING):
+        fetch(b).start()
 
     _, slot, place, _ = row_places((1, rows_n), 1, (x, y, z), readers, owner, lengths)
     wide = lax.broadcasted_iota(jnp.int32, (HOLDERS * MAIN, rows_n), 0)
@@ -92,7 +123,7 @@
         tail = tail + dot(one_hot(wide == tail_at), q[:, cols])
     send[:, PER * MAIN:, :] = tail.astype(BF16).reshape(HOLDERS, MAIN, HEAD)
 
-    pl.semaphore_wait(barrier, HOLDERS - 1)
+    pl.semaphore_wait(barrier, HOLDERS - 1 + 3)
 
     def dispatch(d):
         return pltpu.make_async_remote_copy(
@@ -124,6 +155,8 @@
 
     lax.fori_loop(1, HOLDERS, start_dispatch, 0)
     recv[0] = send[0]
+    for b in range(RING):
+        swap(b).start()
 
     at, slot, place, first = row_places((rows_n, 1), 0, (x, y, z), readers, owner, lengths)
     other = lax.broadcasted_iota(jnp.int32, (rows_n, rows_n), 1)
@@ -162,8 +195,8 @@
         back[low:low + GROUP] = (o[:, :HEAD] / total).astype(BF16).reshape(GROUP, SLOT, HEAD)
         lse = top * FACTOR + jnp.log2(total)
         for i in range(GROUP):
-            part = lse[i * SLOT:(i + 1) * SLOT]
-            lback[low + i] = jnp.sum(jnp.where(lane == sub, part, 0.0), axis=0, keepdims=True)
+            piece_l = lse[i * SLOT:(i + 1) * SLOT]
+            lback[low + i] = jnp.sum(jnp.where(lane == sub, piece_l, 0.0), axis=0, keepdims=True)
 
         def start_give(d, carry):
             give(d).start()
@@ -207,9 +240,59 @@
         top = jnp.maximum(l_pre, l_suf)
         pre_f, suf_f = jnp.exp2(l_pre - top), jnp.exp2(l_suf - top)
         total = pre_f + suf_f * suft[k, :, 1:2]
-        out[:, k * HEAD:(k + 1) * HEAD] = (
+        att[:, k * HEAD:(k + 1) * HEAD] = (
             (pre * pre_f + sufw[k] * suf_f) / total
         ).astype(BF16)
+
+    share = pltpu.make_async_remote_copy(
+        src_ref=att, dst_ref=att_sib, send_sem=att_send, recv_sem=att_recv,
+        device_id={"tp": sibling}, device_id_type=pl.DeviceIdType.MESH,
+    )
+    share.start()
+    for b in range(RING):
+        fetch(b).wait()
+        swap(b).wait()
+    share.wait()
+
+    half = rows_n // 2
+    piece = half // PIECES
+
+    def project(b, low, count):
+        rows = slice(low, low + count)
+        return dot(att[rows, :], w_own[b]) + dot(att_sib[rows, :], w_sib[b])
+
+    def hop(way, step, i):
+        return pltpu.make_async_remote_copy(
+            src_ref=going.at[way, step, i], dst_ref=coming.at[way, step, i],
+            send_sem=go_sem.at[way, step, i], recv_sem=come_sem.at[way, step, i],
+            device_id={"tp": beside[way]}, device_id_type=pl.DeviceIdType.MESH,
+        )
+
+    before, after, across = (h + RING - 1) % RING, (h + 1) % RING, (h + 2) % RING
+    for way, b in ((0, before), (1, after)):
+        first_part = project(b, way * half, half).astype(BF16)
+        for i in range(PIECES):
+            going[way, 0, i] = first_part[i * piece:(i + 1) * piece]
+            hop(way, 0, i).start()
+    part[0] = project(across, 0, rows_n)
+    part[1, :half] = project(after, 0, half)
+    part[1, half:] = project(before, half, half)
+    part[2] = project(h, 0, rows_n)
+    for step in range(HOPS):
+        for i in range(PIECES):
+            for way in range(2):
+                hop(way, step, i).wait_recv()
+                low = way * half + i * piece
+                total = coming[way, step, i].astype(F32) + part[step, low:low + piece]
+                if step < HOPS - 1:
+                    going[way, step + 1, i] = total.astype(BF16)
+                    hop(way, step + 1, i).start()
+                else:
+                    out[low:low + piece] = total.astype(BF16)
+    for way in range(2):
+        for step in range(HOPS):
+            for i in range(PIECES):
+                hop(way, step, i).wait_send()
 
     def finish(d, carry):
         dispatch(d).wait_send()
@@ -220,8 +303,12 @@
     lax.fori_loop(1, HOLDERS, finish, 0)
 
 
-def attend(queries, suffix_kv, cache, readers, owner, lengths):
-    rows_n = queries.shape[0]
+def attend(queries, suffix_kv, cache, weight, readers, owner, lengths):
+    rows_n, width = queries.shape
+    wide_out = weight.shape[1] // (RING * CORES)
+    moved = pltpu.VMEM((2, HOPS, PIECES, rows_n // 2 // PIECES, wide_out), BF16)
+    moved_sem = pltpu.SemaphoreType.DMA((2, HOPS, PIECES))
+    block_sem = pltpu.SemaphoreType.DMA((RING,))
     vmem = pl.BlockSpec(memory_space=pltpu.VMEM)
     smem = pl.BlockSpec(memory_space=pltpu.SMEM)
     dma = pltpu.SemaphoreType.DMA((HOLDERS,))
@@ -229,14 +316,23 @@
     lses = pltpu.VMEM((HOLDERS, 1, HEAD), F32)
     return pl.pallas_call(
         attend_kernel,
-        out_shape=jax.ShapeDtypeStruct(queries.shape, BF16),
-        in_specs=[vmem, vmem, vmem, smem, smem, smem],
+        out_shape=jax.ShapeDtypeStruct((rows_n, wide_out), BF16),
+        in_specs=[vmem, vmem, vmem, pl.BlockSpec(memory_space=pl.ANY), smem, smem, smem],
         out_specs=vmem,
         scratch_shapes=[
             slots, slots, slots, slots, lses, lses,
             pltpu.VMEM((PER, rows_n, HEAD), F32),
             pltpu.VMEM((PER, rows_n, HEAD), F32),
+            pltpu.VMEM((RING, width, wide_out), BF16),
+            pltpu.VMEM((RING, width, wide_out), BF16),
+            pltpu.VMEM((rows_n, width), BF16),
+            pltpu.VMEM((rows_n, width), BF16),
+            pltpu.VMEM((HOPS, rows_n, wide_out), F32),
+            moved, moved,
             dma, dma, dma, dma, dma, dma,
+            block_sem, block_sem, block_sem,
+            pltpu.SemaphoreType.DMA, pltpu.SemaphoreType.DMA,
+            moved_sem, moved_sem,
         ],
         compiler_params=pltpu.CompilerParams(
             collective_id=0, has_side_effects=True, vmem_limit_bytes=56 * 1024 * 1024
@@ -247,13 +343,11 @@
             transcendentals=HOLDERS * SLOT * cache.shape[2],
         ),
         name="attend",
-    )(queries, suffix_kv, cache, readers, owner, lengths)
+    )(queries, suffix_kv, cache, weight, readers, owner, lengths)
 
 
 def local(queries, suffix_kv, prefix_cache, out_weight, readers, owner, lengths):
-    attention = attend(queries, suffix_kv, prefix_cache, readers, owner, lengths)
-    partial = jnp.dot(attention, out_weight, preferred_element_type=F32)
-    return lax.psum_scatter(partial.astype(BF16), "tp", scatter_dimension=1, tiled=True)
+    return attend(queries, suffix_kv, prefix_cache, out_weight, readers, owner, lengths)
 
 
 def solution(mesh):

time: 117 us -> 80.6 us (0.69)
  waiting for transfers between devices: 61.2 us -> 0 us
  Pallas kernels: 33.7 us -> 78.6 us
  between operations: 13.4 us -> 0.01 us
  matrix products: 7.77 us -> 0 us
  local copies, waits for them, and re-layouts: 0 us -> 1.87 us
    reduce_scatter x1 -> x0, waiting for transfers between devices: 61.2 us -> none  [local(): lax.psum_scatter(partial.astype(BF16), 'tp', scatter_dimension=1, tiled=T...]
    pallas_call x1, Pallas kernels: 33.7 us -> 78.6 us  [attend(): pl.pallas_call(attend_kernel, out_shape=jax.ShapeDtypeStruct((rows_n, wid...]
    dot_general x1 -> x0, matrix products: 7.77 us -> none  [local(): partial = jnp.dot(attention, out_weight, preferred_element_type=F32)]
    unnamed x0 -> x1, local copies, waits for them, and re-layouts: none -> 1.87 us
  transfers between devices with their start and end apart: 1 -> 0, of which waited for: 1 -> 0; matrix products, arithmetic and copies ran while one was open for 0% -> 0% of each run, Pallas kernels for 0% -> 0%
where the time goes in v2:
time: 80.6 us; the launch traced here: 80.5 us
  Pallas kernels  78.6 us (98%)
  local copies, waits for them, and re-layouts  1.87 us (2%)
    pallas_call x1, Pallas kernels, attend(): pl.pallas_call(attend_kernel, out_shape=jax.ShapeDtypeStruct((rows_n, wid...  78.6 us
    unnamed x1, local copies, waits for them, and re-layouts  1.87 us

profile of v2, /device:TPU:1, one launch (start us, length us, event | category | flops | bytes accessed | tf_op | source)
XLA Modules:
  0.0 80.5 jit_solution(3105181159719185848)
XLA Ops:
  0.0 78.6 %attend.1 = bf16[256,1024]{1,0:T(8,128)(2,1)} custom-call(bf16[256,512]{1,0:T(8,128)(2,1)} %q.1, bf16[256,2,128]{2,1,0:T(2,128)(2,1)} %kv.1, bf16[1,2,1536,128]{3,2,1,0:T(8,128)(2,1)} %cache.1, bf16[512,8192]{1,0:T(8,128)(2,1)} %weight.1, s32[1,16]{1,0:T(1,128)} %readers.1, s32[32]{0:T(128)} %owner.1, s32[1,16]{1,0:T(1,128)} %lengths.1), custom_call_target="tpu_custom_call" | custom-call | flops 2013265920 | bytes 4194304 | tf_op jit(solution)/shard_map/attend/pallas_call | solution.py:317
  78.6 1.9 %copy.9 = bf16[256,1024]{1,0:T(8,128)(2,1)} copy(bf16[256,1024]{1,0:T(8,128)(2,1)} %attend.1) | data formatting | bytes 1048576

commit v3 on v1

--- a/solution.py
+++ b/solution.py
@@ -16,6 +16,12 @@
 NX, NY, NZ = 4, 4, 2
 HOLDERS = NX * NY * NZ
 GROUP = 8
+RING = 4
+CORES = 2
+PIECES = 4
+HALVES = 2
+CHIPS = RING * NZ
+SHARE = 32
 NEG = -1e30
 FACTOR = math.log2(math.e) / math.sqrt(HEAD)
 F32 = jnp.float32
@@ -61,13 +67,29 @@
 
 
 def attend_kernel(
-    q, kv, cache, readers, owner, lengths, out,
+    q, kv, cache, weight, readers, owner, lengths, out,
     send, recv, back, ret, lback, lret, sufw, suft,
+    w_own, w_far, att, acc, ship, got,
     send_sem, recv_sem, back_sem, ret_sem, lback_sem, lret_sem,
+    own_sem, sib_send, sib_recv, far_send, far_recv, ring_send, ring_recv,
+    hop_send, hop_recv, core_send, core_recv, ship_send, ship_recv,
 ):
     me = lax.axis_index("grp")
     x, y, z = me // (NY * NZ), (me // NZ) % NY, me % NZ
+    tp = lax.axis_index("tp")
+    h, core = tp // CORES, tp % CORES
+    sibling = h * CORES + 1 - core
+    side = 1 - 2 * z
+    partner = x * (NY * NZ) + y * NZ + 1 - z
+    outer = (h * NZ + z + CHIPS - side) % CHIPS
+    chip = [
+        {"grp": partner, "tp": tp},
+        {"grp": x * (NY * NZ) + y * NZ + outer % NZ, "tp": (outer // NZ) * CORES + core},
+    ]
     rows_n = q.shape[0]
+    wide_out = out.shape[1]
+    pair_out = wide_out // NZ
+    half_out = pair_out // HALVES
 
     barrier = pltpu.get_barrier_semaphore()
 
@@ -79,6 +101,82 @@
         return carry
 
     lax.fori_loop(1, HOLDERS, greet, 0)
+    for d in range(1, RING * CORES):
+        pl.semaphore_signal(
+            barrier, inc=1, device_id={"tp": (tp + d) % (RING * CORES)},
+            device_id_type=pl.DeviceIdType.MESH,
+        )
+
+    pl.semaphore_signal(
+        barrier, inc=1, device_id=chip[1], device_id_type=pl.DeviceIdType.MESH
+    )
+
+    def columns(b, of_core):
+        return pl.multiple_of((b * CORES + of_core) * wide_out + z * pair_out, pair_out)
+
+    def to(device, src, dst, send, recv):
+        return pltpu.make_async_remote_copy(
+            src_ref=src, dst_ref=dst, send_sem=send, recv_sem=recv,
+            device_id=device, device_id_type=pl.DeviceIdType.MESH,
+        )
+
+    fetch_own = pltpu.make_async_copy(
+        weight.at[:, pl.ds(columns(h, core), pair_out)], w_own.at[0], own_sem
+    )
+    fetch_own.start()
+    give_own = to(
+        {"tp": sibling}, weight.at[:, pl.ds(columns(h, 1 - core), pair_out)], w_own.at[1],
+        sib_send, sib_recv,
+    )
+    cores = (core, 1 - core)
+
+    def far(j, r, half):
+        target = (h + RING - side * j) % RING
+        rows = pl.ds(pl.multiple_of((x * NY + y) * SHARE, SHARE), SHARE)
+        first = pl.multiple_of(columns(target, cores[r]) + half * half_out, half_out)
+        return to(
+            {"tp": target * CORES + cores[r]}, weight.at[rows, pl.ds(first, half_out)],
+            w_far.at[half, (j - 1) * CORES + r, x, y],
+            far_send.at[j - 1, r, half], far_recv.at[j - 1, r, half],
+        )
+
+    def ring(half, second, stage, way):
+        step = 1 if way == 0 else 3
+        back_by = (3 if way == 0 else 1) * stage
+        along_x = (half == 0) == (second == 1)
+        if along_x:
+            bx, by = (x + back_by) % NX, y
+            target = ((x + step) % NX) * (NY * NZ) + y * NZ + z
+        else:
+            bx, by = x, (y + back_by) % NY
+            target = x * (NY * NZ) + ((y + step) % NY) * NZ + z
+        some = pl.ds(2 * way, 2)
+        if second == 0:
+            block = w_far.at[half, :, bx, by]
+            if stage == 1:
+                block = w_far.at[half, :, bx, by, pl.ds(way * (SHARE // 2), SHARE // 2)]
+        elif along_x:
+            block = w_far.at[half, :, bx, some] if stage == 1 else w_far.at[half, :, bx]
+        else:
+            block = w_far.at[half, :, some, by] if stage == 1 else w_far.at[half, :, :, by]
+        return to(
+            {"grp": target}, block, block,
+            ring_send.at[half, second, stage, way], ring_recv.at[half, second, stage, way],
+        )
+
+    ways = [(half, way) for half in range(HALVES) for way in range(2)]
+
+    def ring_start(second, stage):
+        for half, way in ways:
+            ring(half, second, stage, way).start()
+
+    def ring_wait(second, stage):
+        for half, way in ways:
+            ring(half, second, stage, way).wait_recv()
+
+    shares = [
+        (j, r, half) for j in range(1, RING) for r in range(CORES) for half in range(HALVES)
+    ]
 
     _, slot, place, _ = row_places((1, rows_n), 1, (x, y, z), readers, owner, lengths)
     wide = lax.broadcasted_iota(jnp.int32, (HOLDERS * MAIN, rows_n), 0)
@@ -92,7 +190,7 @@
         tail = tail + dot(one_hot(wide == tail_at), q[:, cols])
     send[:, PER * MAIN:, :] = tail.astype(BF16).reshape(HOLDERS, MAIN, HEAD)
 
-    pl.semaphore_wait(barrier, HOLDERS - 1)
+    pl.semaphore_wait(barrier, HOLDERS - 1 + RING * CORES)
 
     def dispatch(d):
         return pltpu.make_async_remote_copy(
@@ -124,6 +222,9 @@
 
     lax.fori_loop(1, HOLDERS, start_dispatch, 0)
     recv[0] = send[0]
+    for j, r, half in shares:
+        far(j, r, half).start()
+    give_own.start()
 
     at, slot, place, first = row_places((rows_n, 1), 0, (x, y, z), readers, owner, lengths)
     other = lax.broadcasted_iota(jnp.int32, (rows_n, rows_n), 1)
@@ -162,8 +263,8 @@
         back[low:low + GROUP] = (o[:, :HEAD] / total).astype(BF16).reshape(GROUP, SLOT, HEAD)
         lse = top * FACTOR + jnp.log2(total)
         for i in range(GROUP):
-            part = lse[i * SLOT:(i + 1) * SLOT]
-            lback[low + i] = jnp.sum(jnp.where(lane == sub, part, 0.0), axis=0, keepdims=True)
+            piece_l = lse[i * SLOT:(i + 1) * SLOT]
+            lback[low + i] = jnp.sum(jnp.where(lane == sub, piece_l, 0.0), axis=0, keepdims=True)
 
         def start_give(d, carry):
             give(d).start()
@@ -171,6 +272,13 @@
             return carry
 
         lax.fori_loop(max(low, 1), low + GROUP, start_give, 0)
+        if a == 1:
+            for j, r, half in shares:
+                far(j, r, half).wait_recv()
+            ring_start(0, 0)
+        if a == 3:
+            ring_wait(0, 0)
+            ring_start(0, 1)
 
     ret[0] = back[0]
     lret[0] = lback[0]
@@ -187,6 +295,8 @@
         return carry
 
     lax.fori_loop(1, HOLDERS, wait_ret, 0)
+    ring_wait(0, 1)
+    ring_start(1, 0)
 
     l_all = lret[...].reshape(HOLDERS, HEAD)
     l_high = l_all.astype(BF16)
@@ -207,9 +317,90 @@
         top = jnp.maximum(l_pre, l_suf)
         pre_f, suf_f = jnp.exp2(l_pre - top), jnp.exp2(l_suf - top)
         total = pre_f + suf_f * suft[k, :, 1:2]
-        out[:, k * HEAD:(k + 1) * HEAD] = (
+        att[0, 0, :, k * HEAD:(k + 1) * HEAD] = (
             (pre * pre_f + sufw[k] * suf_f) / total
         ).astype(BF16)
+
+    piece = rows_n // PIECES
+
+    def rows_of(i):
+        return pl.ds(i * piece, piece)
+
+    def hop(way, k, i):
+        if way == 0:
+            src, dst = (0, 4, 5)[k], k + 1
+        else:
+            src, dst = k, k + 4
+        return to(
+            chip[way], att.at[src, 0, rows_of(i)], att.at[dst, 0, rows_of(i)],
+            hop_send.at[way, k, i], hop_recv.at[way, k, i],
+        )
+
+    def across(b, i):
+        return to(
+            {"tp": sibling}, att.at[b, 0, rows_of(i)], att.at[b, 1, rows_of(i)],
+            core_send.at[b, i], core_recv.at[b, i],
+        )
+
+    def weight_of(j, r):
+        if j == 0:
+            return w_own[r]
+        return jnp.concatenate(
+            [
+                w_far[half, (j - 1) * CORES + r].reshape(q.shape[1], half_out)
+                for half in range(HALVES)
+            ],
+            axis=1,
+        )
+
+    def project(b, j):
+        return dot(att[b, 0], weight_of(j, 0)) + dot(att[b, 1], weight_of(j, 1))
+
+    def arrived(b):
+        for i in range(PIECES):
+            across(b, i).wait_recv()
+
+    for i in range(PIECES):
+        for way in range(2):
+            hop(way, 0, i).start()
+    for i in range(PIECES):
+        across(0, i).start()
+    fetch_own.wait()
+    give_own.wait_recv()
+    arrived(0)
+    acc[0] = project(0, 0)
+    for k in range(RING):
+        for i in range(PIECES):
+            for way in (1, 0):
+                if way == 0 and k == RING - 1:
+                    continue
+                hop(way, k, i).wait_recv()
+                if way == 0:
+                    hop(1, k + 1, i).start()
+                elif k < 2:
+                    hop(0, k + 1, i).start()
+                across(k + 1 if way == 0 else k + 4, i).start()
+        if k == 0:
+            ring_wait(1, 0)
+            ring_start(1, 1)
+            arrived(1)
+            acc[1] = project(1, 0)
+        if k == 2:
+            ring_wait(1, 1)
+            for b in (3, 4, 6):
+                arrived(b)
+            ship[...] = (acc[1] + project(3, 1) + project(4, 3) + project(6, 2)).astype(BF16)
+            back_rows = to({"grp": partner}, ship, got, ship_send, ship_recv)
+            back_rows.start()
+            arrived(2)
+            arrived(5)
+            acc[0] = acc[0] + project(2, 1) + project(5, 3)
+    arrived(7)
+    mine = pl.multiple_of(z * pair_out, pair_out)
+    other = pl.multiple_of((1 - z) * pair_out, pair_out)
+    out[:, pl.ds(mine, pair_out)] = (acc[0] + project(7, 2)).astype(BF16)
+    back_rows.wait()
+    out[:, pl.ds(other, pair_out)] = got[...]
 
     def finish(d, carry):
         dispatch(d).wait_send()
@@ -218,25 +409,57 @@
         return carry
 
     lax.fori_loop(1, HOLDERS, finish, 0)
-
-
-def attend(queries, suffix_kv, cache, readers, owner, lengths):
-    rows_n = queries.shape[0]
+    give_own.wait_send()
+    for j, r, half in shares:
+        far(j, r, half).wait_send()
+    for half, way in ways:
+        for second in range(2):
+            for stage in range(2):
+                ring(half, second, stage, way).wait_send()
+    for i in range(PIECES):
+        for k in range(RING):
+            if k < RING - 1:
+                hop(0, k, i).wait_send()
+            hop(1, k, i).wait_send()
+        for b in range(CHIPS):
+            across(b, i).wait_send()
+
+
+def attend(queries, suffix_kv, cache, weight, readers, owner, lengths):
+    rows_n, width = queries.shape
+    wide_out = weight.shape[1] // (RING * CORES)
+    pair_out = wide_out // NZ
     vmem = pl.BlockSpec(memory_space=pltpu.VMEM)
     smem = pl.BlockSpec(memory_space=pltpu.SMEM)
-    dma = pltpu.SemaphoreType.DMA((HOLDERS,))
+    sems = pltpu.SemaphoreType.DMA
+    dma = sems((HOLDERS,))
+    one = sems
     slots = pltpu.VMEM((HOLDERS, SLOT, HEAD), BF16)
     lses = pltpu.VMEM((HOLDERS, 1, HEAD), F32)
     return pl.pallas_call(
         attend_kernel,
-        out_shape=jax.ShapeDtypeStruct(queries.shape, BF16),
-        in_specs=[vmem, vmem, vmem, smem, smem, smem],
+        out_shape=jax.ShapeDtypeStruct((rows_n, wide_out), BF16),
+        in_specs=[vmem, vmem, vmem, pl.BlockSpec(memory_space=pl.ANY), smem, smem, smem],
         out_specs=vmem,
         scratch_shapes=[
             slots, slots, slots, slots, lses, lses,
             pltpu.VMEM((PER, rows_n, HEAD), F32),
             pltpu.VMEM((PER, rows_n, HEAD), F32),
+            pltpu.VMEM((CORES, width, pair_out), BF16),
+            pltpu.VMEM(
+                (HALVES, (RING - 1) * CORES, NX, NY, SHARE, pair_out // HALVES), BF16
+            ),
+            pltpu.VMEM((CHIPS, CORES, rows_n, width), BF16),
+            pltpu.VMEM((2, rows_n, pair_out), F32),
+            pltpu.VMEM((rows_n, pair_out), BF16),
+            pltpu.VMEM((rows_n, pair_out), BF16),
             dma, dma, dma, dma, dma, dma,
+            one, one, one,
+            sems((RING - 1, CORES, HALVES)), sems((RING - 1, CORES, HALVES)),
+            sems((HALVES, 2, 2, 2)), sems((HALVES, 2, 2, 2)),
+            sems((2, RING, PIECES)), sems((2, RING, PIECES)),
+            sems((CHIPS, PIECES)), sems((CHIPS, PIECES)),
+            one, one,
         ],
         compiler_params=pltpu.CompilerParams(
             collective_id=0, has_side_effects=True, vmem_limit_bytes=56 * 1024 * 1024
@@ -247,13 +470,11 @@
             transcendentals=HOLDERS * SLOT * cache.shape[2],
         ),
         name="attend",
-    )(queries, suffix_kv, cache, readers, owner, lengths)
+    )(queries, suffix_kv, cache, weight, readers, owner, lengths)
 
 
 def local(queries, suffix_kv, prefix_cache, out_weight, readers, owner, lengths):
-    attention = attend(queries, suffix_kv, prefix_cache, readers, owner, lengths)
-    partial = jnp.dot(attention, out_weight, preferred_element_type=F32)
-    return lax.psum_scatter(partial.astype(BF16), "tp", scatter_dimension=1, tiled=True)
+    return attend(queries, suffix_kv, prefix_cache, out_weight, readers, owner, lengths)
 
 
 def solution(mesh):

time: 117 us -> 78.4 us (0.67)
  waiting for transfers between devices: 61.2 us -> 0 us
  Pallas kernels: 33.7 us -> 76.4 us
  between operations: 13.4 us -> 0.01 us
  matrix products: 7.77 us -> 0 us
  local copies, waits for them, and re-layouts: 0 us -> 1.87 us
    reduce_scatter x1 -> x0, waiting for transfers between devices: 61.2 us -> none  [local(): lax.psum_scatter(partial.astype(BF16), 'tp', scatter_dimension=1, tiled=T...]
    pallas_call x1, Pallas kernels: 33.7 us -> 76.4 us  [attend(): pl.pallas_call(attend_kernel, out_shape=jax.ShapeDtypeStruct((rows_n, wid...]
    dot_general x1 -> x0, matrix products: 7.77 us -> none  [local(): partial = jnp.dot(attention, out_weight, preferred_element_type=F32)]
    unnamed x0 -> x1, local copies, waits for them, and re-layouts: none -> 1.87 us
  transfers between devices with their start and end apart: 1 -> 0, of which waited for: 1 -> 0; matrix products, arithmetic and copies ran while one was open for 0% -> 0% of each run, Pallas kernels for 0% -> 0%
where the time goes in v3:
time: 78.4 us; the launch traced here: 78.3 us
  Pallas kernels  76.4 us (97%)
  local copies, waits for them, and re-layouts  1.87 us (2%)
    pallas_call x1, Pallas kernels, attend(): pl.pallas_call(attend_kernel, out_shape=jax.ShapeDtypeStruct((rows_n, wid...  76.4 us
    unnamed x1, local copies, waits for them, and re-layouts  1.87 us

profile of v3, /device:TPU:1, one launch (start us, length us, event | category | flops | bytes accessed | tf_op | source)
XLA Modules:
  0.0 78.3 jit_solution(17672037209867749591)
XLA Ops:
  0.0 76.4 %attend.1 = bf16[256,1024]{1,0:T(8,128)(2,1)} custom-call(bf16[256,512]{1,0:T(8,128)(2,1)} %q.1, bf16[256,2,128]{2,1,0:T(2,128)(2,1)} %kv.1, bf16[1,2,1536,128]{3,2,1,0:T(8,128)(2,1)} %cache.1, bf16[512,8192]{1,0:T(8,128)(2,1)} %weight.1, s32[1,16]{1,0:T(1,128)} %readers.1, s32[32]{0:T(128)} %owner.1, s32[1,16]{1,0:T(1,128)} %lengths.1), custom_call_target="tpu_custom_call" | custom-call | flops 2013265920 | bytes 4194304 | tf_op jit(solution)/shard_map/attend/pallas_call | solution.py:439
  76.4 1.9 %copy.9 = bf16[256,1024]{1,0:T(8,128)(2,1)} copy(bf16[256,1024]{1,0:T(8,128)(2,1)} %attend.1) | data formatting | bytes 1048576

commit v4 on v3

--- a/solution.py
+++ b/solution.py
@@ -15,10 +15,11 @@
 SLOT = MOST * PER
 NX, NY, NZ = 4, 4, 2
 HOLDERS = NX * NY * NZ
-GROUP = 8
+GROUP = 4
+ORDER = (5, 4, 3, 7, 2, 6, 1, 0)
 RING = 4
 CORES = 2
-PIECES = 4
+PIECES = 2
 HALVES = 2
 CHIPS = RING * NZ
 SHARE = 32
@@ -67,7 +68,8 @@
 
 
 def attend_kernel(
-    q, kv, cache, weight, readers, owner, lengths, out,
+    q_in, kv_in, cache_in, weight, readers, owner, lengths, out,
+    q, kv, cache, in_sem,
     send, recv, back, ret, lback, lret, sufw, suft,
     w_own, w_far, att, acc, ship, got,
     send_sem, recv_sem, back_sem, ret_sem, lback_sem, lret_sem,
@@ -91,6 +93,12 @@
     pair_out = wide_out // NZ
     half_out = pair_out // HALVES
 
+    loads = [
+        pltpu.make_async_copy(src, dst, in_sem.at[i])
+        for i, (src, dst) in enumerate(((q_in, q), (kv_in, kv), (cache_in, cache)))
+    ]
+    for load in loads:
+        load.start()
     barrier = pltpu.get_barrier_semaphore()
 
     def greet(d, carry):
@@ -178,6 +186,7 @@
         (j, r, half) for j in range(1, RING) for r in range(CORES) for half in range(HALVES)
     ]
 
+    loads[0].wait()
     _, slot, place, _ = row_places((1, rows_n), 1, (x, y, z), readers, owner, lengths)
     wide = lax.broadcasted_iota(jnp.int32, (HOLDERS * MAIN, rows_n), 0)
     main_at = jnp.where(place < MAIN, slot * MAIN + place, -1)
@@ -216,16 +225,14 @@
             device_id_type=pl.DeviceIdType.MESH,
         )
 
-    def start_dispatch(d, carry):
-        dispatch(d).start()
-        return carry
-
-    lax.fori_loop(1, HOLDERS, start_dispatch, 0)
+    for a in ORDER:
+        for d in range(max(a * GROUP, 1), (a + 1) * GROUP):
+            dispatch(d).start()
     recv[0] = send[0]
-    for j, r, half in shares:
-        far(j, r, half).start()
     give_own.start()
 
+    loads[1].wait()
+    loads[2].wait()
     at, slot, place, first = row_places((rows_n, 1), 0, (x, y, z), readers, owner, lengths)
     other = lax.broadcasted_iota(jnp.int32, (rows_n, rows_n), 1)
     visible = (other >= first) & (other <= at)
@@ -246,14 +253,11 @@
     )
     lane = lax.broadcasted_iota(jnp.int32, (SLOT, HEAD), 1)
     sub = lax.broadcasted_iota(jnp.int32, (SLOT, HEAD), 0)
-    for a in range(HOLDERS // GROUP):
+    for turn, a in enumerate(ORDER):
         low = a * GROUP
 
-        def wait_slot(d, carry):
+        for d in range(max(low, 1), low + GROUP):
             dispatch(d).wait_recv()
-            return carry
-
-        lax.fori_loop(max(low, 1), low + GROUP, wait_slot, 0)
         block = recv[low:low + GROUP].reshape(GROUP * SLOT, HEAD)
         s = dot_t(block, prefix_keys)
         top = jnp.max(s, axis=1, keepdims=True)
@@ -266,19 +270,12 @@
             piece_l = lse[i * SLOT:(i + 1) * SLOT]
             lback[low + i] = jnp.sum(jnp.where(lane == sub, piece_l, 0.0), axis=0, keepdims=True)
 
-        def start_give(d, carry):
+        for d in range(max(low, 1), low + GROUP):
             give(d).start()
             give_l(d).start()
-            return carry
-
-        lax.fori_loop(max(low, 1), low + GROUP, start_give, 0)
-        if a == 1:
+        if turn == 0:
             for j, r, half in shares:
-                far(j, r, half).wait_recv()
-            ring_start(0, 0)
-        if a == 3:
-            ring_wait(0, 0)
-            ring_start(0, 1)
+                far(j, r, half).start()
 
     ret[0] = back[0]
     lret[0] = lback[0]
@@ -295,8 +292,9 @@
         return carry
 
     lax.fori_loop(1, HOLDERS, wait_ret, 0)
-    ring_wait(0, 1)
-    ring_start(1, 0)
+    for j, r, half in shares:
+        far(j, r, half).wait_recv()
+    ring_start(0, 0)
 
     l_all = lret[...].reshape(HOLDERS, HEAD)
     l_high = l_all.astype(BF16)
@@ -365,6 +363,8 @@
             hop(way, 0, i).start()
     for i in range(PIECES):
         across(0, i).start()
+    ring_wait(0, 0)
+    ring_start(0, 1)
     fetch_own.wait()
     give_own.wait_recv()
     arrived(0)
@@ -381,14 +381,17 @@
                     hop(0, k + 1, i).start()
                 across(k + 1 if way == 0 else k + 4, i).start()
         if k == 0:
+            ring_wait(0, 1)
+            ring_start(1, 0)
+            arrived(1)
+            acc[1] = project(1, 0)
+        if k == 1:
             ring_wait(1, 0)
             ring_start(1, 1)
-            arrived(1)
-            acc[1] = project(1, 0)
         if k == 2:
-            ring_wait(1, 1)
             for b in (3, 4, 6):
                 arrived(b)
+            ring_wait(1, 1)
             ship[...] = (acc[1] + project(3, 1) + project(4, 3) + project(6, 2)).astype(BF16)
             back_rows = to({"grp": partner}, ship, got, ship_send, ship_recv)
             back_rows.start()
@@ -431,6 +434,7 @@
     pair_out = wide_out // NZ
     vmem = pl.BlockSpec(memory_space=pltpu.VMEM)
     smem = pl.BlockSpec(memory_space=pltpu.SMEM)
+    anywhere = pl.BlockSpec(memory_space=pl.ANY)
     sems = pltpu.SemaphoreType.DMA
     dma = sems((HOLDERS,))
     one = sems
@@ -438,10 +442,12 @@
     lses = pltpu.VMEM((HOLDERS, 1, HEAD), F32)
     return pl.pallas_call(
         attend_kernel,
-        out_shape=jax.ShapeDtypeStruct((rows_n, wide_out), BF16),
-        in_specs=[vmem, vmem, vmem, pl.BlockSpec(memory_space=pl.ANY), smem, smem, smem],
+        out_shape=pltpu.VMEM((rows_n, wide_out), BF16),
+        in_specs=[anywhere, anywhere, anywhere, anywhere, smem, smem, smem],
         out_specs=vmem,
         scratch_shapes=[
+            pltpu.VMEM(queries.shape, BF16), pltpu.VMEM(suffix_kv.shape, BF16),
+            pltpu.VMEM(cache.shape, BF16), sems((3,)),
             slots, slots, slots, slots, lses, lses,
             pltpu.VMEM((PER, rows_n, HEAD), F32),
             pltpu.VMEM((PER, rows_n, HEAD), F32),

time: 78.4 us -> 68 us (0.87); the launches traced: 78.3 us -> 67 us
  Pallas kernels: 76.4 us -> 66.2 us
  local copies, waits for them, and re-layouts: 1.87 us -> 0.8 us
    pallas_call x1, Pallas kernels: 76.4 us -> 66.2 us  [attend(): pl.pallas_call(attend_kernel, out_shape=pltpu.VMEM((rows_n, wide_out), BF...]
    unnamed x1, local copies, waits for them, and re-layouts: 1.87 us -> 0.8 us
where the time goes in v4:
time: 68 us; the launch traced here: 67 us
  Pallas kernels  66.2 us (97%)
  local copies, waits for them, and re-layouts  0.8 us (1%)
    pallas_call x1, Pallas kernels, attend(): pl.pallas_call(attend_kernel, out_shape=pltpu.VMEM((rows_n, wide_out), BF...  66.2 us

profile of v4, /device:TPU:1, one launch (start us, length us, event | category | flops | bytes accessed | tf_op | source)
XLA Modules:
  0.0 67.0 jit_solution(18308427938359319564)
XLA Ops:
  0.0 66.2 %attend.1 = bf16[256,1024]{1,0:T(8,128)(2,1)S(1)} custom-call(bf16[256,512]{1,0:T(8,128)(2,1)} %q_in.1, bf16[256,2,128]{2,1,0:T(2,128)(2,1)} %kv_in.1, bf16[1,2,1536,128]{3,2,1,0:T(8,128)(2,1)} %cache_in.1, bf16[512,8192]{1,0:T(8,128)(2,1)} %weight.1, s32[1,16]{1,0:T(1,128)} %readers.1, s32[32]{0:T(128)} %owner.1, s32[1,16]{1,0:T(1,128)} %lengths.1), custom_call_target="tpu_custom_call" | custom-call | flops 2013265920 | bytes 4194304 | tf_op jit(solution)/shard_map/attend/pallas_call | solution.py:443
  66.2 0.8 %copy.9 = bf16[256,1024]{1,0:T(8,128)(2,1)} copy(bf16[256,1024]{1,0:T(8,128)(2,1)S(1)} %attend.1) | data formatting | bytes 1048576

commit v5 on v4

--- a/solution.py
+++ b/solution.py
@@ -37,13 +37,19 @@
     return lax.dot_general(a, b, (((1,), (1,)), ((), ())), preferred_element_type=F32)
 
 
-def shifted(x, y, z, d, sign):
+def offsets(x, y, z):
+    return (
+        [lax.rem(x + i, NX) * (NY * NZ) for i in range(NX)],
+        [lax.rem(y + i, NY) * NZ for i in range(NY)],
+        [lax.rem(z + i, NZ) for i in range(NZ)],
+    )
+
+
+def shifted(steps, d, sign):
     dx, dy, dz = d // (NY * NZ), (d // NZ) % NY, d % NZ
-    if sign > 0:
-        nx, ny, nz = (x + dx) % NX, (y + dy) % NY, (z + dz) % NZ
-    else:
-        nx, ny, nz = (x + NX - dx) % NX, (y + NY - dy) % NY, (z + NZ - dz) % NZ
-    return nx * (NY * NZ) + ny * NZ + nz
+    if sign < 0:
+        dx, dy, dz = (NX - dx) % NX, (NY - dy) % NY, (NZ - dz) % NZ
+    return steps[0][dx] + steps[1][dy] + steps[2][dz]
 
 
 def row_places(shape, axis, me, readers, owner, lengths):
@@ -69,7 +75,7 @@
 
 def attend_kernel(
     q_in, kv_in, cache_in, weight, readers, owner, lengths, out,
-    q, kv, cache, in_sem,
+    q, kv, cache, from_tail, in_sem,
     send, recv, back, ret, lback, lret, sufw, suft,
     w_own, w_far, att, acc, ship, got,
     send_sem, recv_sem, back_sem, ret_sem, lback_sem, lret_sem,
@@ -88,6 +94,7 @@
         {"grp": partner, "tp": tp},
         {"grp": x * (NY * NZ) + y * NZ + outer % NZ, "tp": (outer // NZ) * CORES + core},
     ]
+    steps = offsets(x, y, z)
     rows_n = q.shape[0]
     wide_out = out.shape[1]
     pair_out = wide_out // NZ
@@ -101,14 +108,14 @@
         load.start()
     barrier = pltpu.get_barrier_semaphore()
 
-    def greet(d, carry):
+    def greet(d):
         pl.semaphore_signal(
-            barrier, inc=1, device_id={"grp": shifted(x, y, z, d, 1)},
+            barrier, inc=1, device_id={"grp": shifted(steps, d, 1)},
             device_id_type=pl.DeviceIdType.MESH,
         )
-        return carry
-
-    lax.fori_loop(1, HOLDERS, greet, 0)
+
+    for d in range(1, HOLDERS):
+        greet(d)
     for d in range(1, RING * CORES):
         pl.semaphore_signal(
             barrier, inc=1, device_id={"tp": (tp + d) % (RING * CORES)},
@@ -141,10 +148,10 @@
     def far(j, r, half):
         target = (h + RING - side * j) % RING
         rows = pl.ds(pl.multiple_of((x * NY + y) * SHARE, SHARE), SHARE)
-        first = pl.multiple_of(columns(target, cores[r]) + half * half_out, half_out)
+        first = columns(target, cores[r])
         return to(
-            {"tp": target * CORES + cores[r]}, weight.at[rows, pl.ds(first, half_out)],
-            w_far.at[half, (j - 1) * CORES + r, x, y],
+            {"tp": target * CORES + cores[r]}, weight.at[rows, pl.ds(first, pair_out)],
+            w_far.at[(j - 1) * CORES + r, x, y],
             far_send.at[j - 1, r, half], far_recv.at[j - 1, r, half],
         )
 
@@ -159,14 +166,15 @@
             bx, by = x, (y + back_by) % NY
             target = x * (NY * NZ) + ((y + step) % NY) * NZ + z
         some = pl.ds(2 * way, 2)
+        cols = pl.ds(half * half_out, half_out)
         if second == 0:
-            block = w_far.at[half, :, bx, by]
+            block = w_far.at[:, bx, by, :, cols]
             if stage == 1:
-                block = w_far.at[half, :, bx, by, pl.ds(way * (SHARE // 2), SHARE // 2)]
+                block = w_far.at[:, bx, by, pl.ds(way * (SHARE // 2), SHARE // 2), cols]
         elif along_x:
-            block = w_far.at[half, :, bx, some] if stage == 1 else w_far.at[half, :, bx]
+            block = w_far.at[:, bx, some, :, cols] if stage == 1 else w_far.at[:, bx, :, :, cols]
         else:
-            block = w_far.at[half, :, some, by] if stage == 1 else w_far.at[half, :, :, by]
+            block = w_far.at[:, some, by, :, cols] if stage == 1 else w_far.at[:, :, by, :, cols]
         return to(
             {"grp": target}, block, block,
             ring_send.at[half, second, stage, way], ring_recv.at[half, second, stage, way],
@@ -183,7 +191,7 @@
             ring(half, second, stage, way).wait_recv()
 
     shares = [
-        (j, r, half) for j in range(1, RING) for r in range(CORES) for half in range(HALVES)
+        (j, r, half) for j in range(1, RING) for r in range(CORES) for half in range(1)
     ]
 
     loads[0].wait()
@@ -205,7 +213,7 @@
         return pltpu.make_async_remote_copy(
             src_ref=send.at[d], dst_ref=recv.at[d],
             send_sem=send_sem.at[d], recv_sem=recv_sem.at[d],
-            device_id={"grp": shifted(x, y, z, d, 1)},
+            device_id={"grp": shifted(steps, d, 1)},
             device_id_type=pl.DeviceIdType.MESH,
         )
 
@@ -213,7 +221,7 @@
         return pltpu.make_async_remote_copy(
             src_ref=back.at[d], dst_ref=ret.at[d],
             send_sem=back_sem.at[d], recv_sem=ret_sem.at[d],
-            device_id={"grp": shifted(x, y, z, d, -1)},
+            device_id={"grp": shifted(steps, d, -1)},
             device_id_type=pl.DeviceIdType.MESH,
         )
 
@@ -221,7 +229,7 @@
         return pltpu.make_async_remote_copy(
             src_ref=lback.at[d], dst_ref=lret.at[d],
             send_sem=lback_sem.at[d], recv_sem=lret_sem.at[d],
-            device_id={"grp": shifted(x, y, z, d, -1)},
+            device_id={"grp": shifted(steps, d, -1)},
             device_id_type=pl.DeviceIdType.MESH,
         )
 
@@ -280,18 +288,36 @@
     ret[0] = back[0]
     lret[0] = lback[0]
 
+    def hop(way, k, i):
+        if way == 0:
+            src, dst = (0, 4, 5)[k], k + 1
+        else:
+            src, dst = k, k + 4
+        return to(
+            chip[way], att.at[src, 0, i], att.at[dst, 0, i],
+            hop_send.at[way, k, i], hop_recv.at[way, k, i],
+        )
+
+    def across(b, i):
+        return to(
+            {"tp": sibling}, att.at[b, 0, i], att.at[b, 1, i],
+            core_send.at[b, i], core_recv.at[b, i],
+        )
+
     cols = lax.broadcasted_iota(jnp.int32, (rows_n, HOLDERS * MAIN), 1)
     from_main = one_hot(cols == jnp.where(place < MAIN, slot * MAIN + place, -1))
     slots = lax.broadcasted_iota(jnp.int32, (rows_n, HOLDERS), 1)
     from_slot = one_hot(slots == slot)
     lanes = lax.broadcasted_iota(jnp.int32, (rows_n, HEAD), 1)
 
-    def wait_ret(d, carry):
+    for k in range(PER):
+        from_tail[k] = one_hot(
+            cols == jnp.where(place >= MAIN, slot * MAIN + TAIL * k + place - MAIN, -1)
+        )
+
+    for d in range(1, HOLDERS):
         give(d).wait_recv()
         give_l(d).wait_recv()
-        return carry
-
-    lax.fori_loop(1, HOLDERS, wait_ret, 0)
     for j, r, half in shares:
         far(j, r, half).wait_recv()
     ring_start(0, 0)
@@ -304,65 +330,38 @@
     l_rows = dot(from_slot, l_high) + dot(from_slot, l_mid) + dot(from_slot, l_low)
     tails = ret[:, PER * MAIN:, :].reshape(HOLDERS * MAIN, HEAD)
     for k in range(PER):
-        from_tail = one_hot(
-            cols == jnp.where(place >= MAIN, slot * MAIN + TAIL * k + place - MAIN, -1)
-        )
         mains = ret[:, k * MAIN:(k + 1) * MAIN, :].reshape(HOLDERS * MAIN, HEAD)
-        pre = dot(from_main, mains) + dot(from_tail, tails)
+        pre = dot(from_main, mains) + dot(from_tail[k], tails)
         l_at = jnp.where(place < MAIN, MAIN * k + place, MAIN * PER + TAIL * k + place - MAIN)
         l_pre = jnp.sum(jnp.where(lanes == l_at, l_rows, 0.0), axis=1, keepdims=True)
         l_suf = suft[k, :, 0:1]
         top = jnp.maximum(l_pre, l_suf)
         pre_f, suf_f = jnp.exp2(l_pre - top), jnp.exp2(l_suf - top)
         total = pre_f + suf_f * suft[k, :, 1:2]
-        att[0, 0, :, k * HEAD:(k + 1) * HEAD] = (
+        i, at_k = k * PIECES // PER, k % (PER // PIECES) * HEAD
+        att[0, 0, i, :, at_k:at_k + HEAD] = (
             (pre * pre_f + sufw[k] * suf_f) / total
         ).astype(BF16)
-
-    piece = rows_n // PIECES
-
-    def rows_of(i):
-        return pl.ds(i * piece, piece)
-
-    def hop(way, k, i):
-        if way == 0:
-            src, dst = (0, 4, 5)[k], k + 1
-        else:
-            src, dst = k, k + 4
-        return to(
-            chip[way], att.at[src, 0, rows_of(i)], att.at[dst, 0, rows_of(i)],
-            hop_send.at[way, k, i], hop_recv.at[way, k, i],
-        )
-
-    def across(b, i):
-        return to(
-            {"tp": sibling}, att.at[b, 0, rows_of(i)], att.at[b, 1, rows_of(i)],
-            core_send.at[b, i], core_recv.at[b, i],
-        )
+        if (k + 1) % (PER // PIECES) == 0:
+            for way in range(2):
+                hop(way, 0, i).start()
+            across(0, i).start()
 
     def weight_of(j, r):
         if j == 0:
             return w_own[r]
-        return jnp.concatenate(
-            [
-                w_far[half, (j - 1) * CORES + r].reshape(q.shape[1], half_out)
-                for half in range(HALVES)
-            ],
-            axis=1,
-        )
+        return w_far[(j - 1) * CORES + r].reshape(q.shape[1], pair_out)
 
     def project(b, j):
-        return dot(att[b, 0], weight_of(j, 0)) + dot(att[b, 1], weight_of(j, 1))
+        rows = [
+            jnp.concatenate([att[b, r, i] for i in range(PIECES)], axis=1) for r in range(CORES)
+        ]
+        return dot(rows[0], weight_of(j, 0)) + dot(rows[1], weight_of(j, 1))
 
     def arrived(b):
         for i in range(PIECES):
             across(b, i).wait_recv()
 
-    for i in range(PIECES):
-        for way in range(2):
-            hop(way, 0, i).start()
-    for i in range(PIECES):
-        across(0, i).start()
     ring_wait(0, 0)
     ring_start(0, 1)
     fetch_own.wait()
@@ -381,6 +380,13 @@
                     hop(0, k + 1, i).start()
                 across(k + 1 if way == 0 else k + 4, i).start()
         if k == 0:
+            for d in range(1, HOLDERS):
+                dispatch(d).wait_send()
+                give(d).wait_send()
+                give_l(d).wait_send()
+            give_own.wait_send()
+            for j, r, half in shares:
+                far(j, r, half).wait_send()
             ring_wait(0, 1)
             ring_start(1, 0)
             arrived(1)
@@ -398,6 +404,17 @@
             arrived(2)
             arrived(5)
             acc[0] = acc[0] + project(2, 1) + project(5, 3)
+            for half, way in ways:
+                for second in range(2):
+                    for stage in range(2):
+                        ring(half, second, stage, way).wait_send()
+            for i in range(PIECES):
+                for n in range(RING - 1):
+                    hop(0, n, i).wait_send()
+                for n in range(2):
+                    hop(1, n, i).wait_send()
+                for b in (0, 1, 2, 4, 5):
+                    across(b, i).wait_send()
     arrived(7)
     mine = pl.multiple_of(z * pair_out, pair_out)
     other = pl.multiple_of((1 - z) * pair_out, pair_out)
@@ -405,26 +422,11 @@
     back_rows.wait()
     out[:, pl.ds(other, pair_out)] = got[...]
 
-    def finish(d, carry):
-        dispatch(d).wait_send()
-        give(d).wait_send()
-        give_l(d).wait_send()
-        return carry
-
-    lax.fori_loop(1, HOLDERS, finish, 0)
-    give_own.wait_send()
-    for j, r, half in shares:
-        far(j, r, half).wait_send()
-    for half, way in ways:
-        for second in range(2):
-            for stage in range(2):
-                ring(half, second, stage, way).wait_send()
+    for k in range(2, RING):
+        for i in range(PIECES):
+            hop(1, k, i).wait_send()
     for i in range(PIECES):
-        for k in range(RING):
-            if k < RING - 1:
-                hop(0, k, i).wait_send()
-            hop(1, k, i).wait_send()
-        for b in range(CHIPS):
+        for b in (3, 6, 7):
             across(b, i).wait_send()
 
 
@@ -447,15 +449,16 @@
         out_specs=vmem,
         scratch_shapes=[
             pltpu.VMEM(queries.shape, BF16), pltpu.VMEM(suffix_kv.shape, BF16),
-            pltpu.VMEM(cache.shape, BF16), sems((3,)),
+            pltpu.VMEM(cache.shape, BF16),
+            pltpu.VMEM((PER, rows_n, HOLDERS * MAIN), BF16), sems((3,)),
             slots, slots, slots, slots, lses, lses,
             pltpu.VMEM((PER, rows_n, HEAD), F32),
             pltpu.VMEM((PER, rows_n, HEAD), F32),
             pltpu.VMEM((CORES, width, pair_out), BF16),
             pltpu.VMEM(
-                (HALVES, (RING - 1) * CORES, NX, NY, SHARE, pair_out // HALVES), BF16
+                ((RING - 1) * CORES, NX, NY, SHARE, pair_out), BF16
             ),
-            pltpu.VMEM((CHIPS, CORES, rows_n, width), BF16),
+            pltpu.VMEM((CHIPS, CORES, PIECES, rows_n, width // PIECES), BF16),
             pltpu.VMEM((2, rows_n, pair_out), F32),
             pltpu.VMEM((rows_n, pair_out), BF16),
             pltpu.VMEM((rows_n, pair_out), BF16),

time: 68 us -> 66.8 us (0.982)
  Pallas kernels: 66.2 us -> 65 us
    pallas_call x1, Pallas kernels: 66.2 us -> 65 us  [attend(): pl.pallas_call(attend_kernel, out_shape=pltpu.VMEM((rows_n, wide_out), BF...]
where the time goes in v5:
time: 66.8 us; the launch traced here: 65.8 us
  Pallas kernels  65 us (97%)
  local copies, waits for them, and re-layouts  0.8 us (1%)
    pallas_call x1, Pallas kernels, attend(): pl.pallas_call(attend_kernel, out_shape=pltpu.VMEM((rows_n, wide_out), BF...  65 us

profile of v5, /device:TPU:1, one launch (start us, length us, event | category | flops | bytes accessed | tf_op | source)
XLA Modules:
  0.0 65.8 jit_solution(10587054281087688197)
XLA Ops:
  0.0 65.0 %attend.1 = bf16[256,1024]{1,0:T(8,128)(2,1)S(1)} custom-call(bf16[256,512]{1,0:T(8,128)(2,1)} %q_in.1, bf16[256,2,128]{2,1,0:T(2,128)(2,1)} %kv_in.1, bf16[1,2,1536,128]{3,2,1,0:T(8,128)(2,1)} %cache_in.1, bf16[512,8192]{1,0:T(8,128)(2,1)} %weight.1, s32[1,16]{1,0:T(1,128)} %readers.1, s32[32]{0:T(128)} %owner.1, s32[1,16]{1,0:T(1,128)} %lengths.1), custom_call_target="tpu_custom_call" | custom-call | flops 2013265920 | bytes 4194304 | tf_op jit(solution)/shard_map/attend/pallas_call | solution.py:445
  65.1 0.8 %copy.9 = bf16[256,1024]{1,0:T(8,128)(2,1)} copy(bf16[256,1024]{1,0:T(8,128)(2,1)S(1)} %attend.1) | data formatting | bytes 1048576

commit v6 on v5

--- a/solution.py
+++ b/solution.py
@@ -16,7 +16,7 @@
 NX, NY, NZ = 4, 4, 2
 HOLDERS = NX * NY * NZ
 GROUP = 4
-ORDER = (5, 4, 3, 7, 2, 6, 1, 0)
+ORDER = (5, 4, 7, 3, 6, 2, 1, 0)
 RING = 4
 CORES = 2
 PIECES = 2
@@ -76,9 +76,9 @@
 def attend_kernel(
     q_in, kv_in, cache_in, weight, readers, owner, lengths, out,
     q, kv, cache, from_tail, in_sem,
-    send, recv, back, ret, lback, lret, sufw, suft,
+    send, recv, back, ret, sufw, suft,
     w_own, w_far, att, acc, ship, got,
-    send_sem, recv_sem, back_sem, ret_sem, lback_sem, lret_sem,
+    send_sem, recv_sem, back_sem, ret_sem,
     own_sem, sib_send, sib_recv, far_send, far_recv, ring_send, ring_recv,
     hop_send, hop_recv, core_send, core_recv, ship_send, ship_recv,
 ):
@@ -225,14 +225,6 @@
             device_id_type=pl.DeviceIdType.MESH,
         )
 
-    def give_l(d):
-        return pltpu.make_async_remote_copy(
-            src_ref=lback.at[d], dst_ref=lret.at[d],
-            send_sem=lback_sem.at[d], recv_sem=lret_sem.at[d],
-            device_id={"grp": shifted(steps, d, -1)},
-            device_id_type=pl.DeviceIdType.MESH,
-        )
-
     for a in ORDER:
         for d in range(max(a * GROUP, 1), (a + 1) * GROUP):
             dispatch(d).start()
@@ -261,6 +253,7 @@
     )
     lane = lax.broadcasted_iota(jnp.int32, (SLOT, HEAD), 1)
     sub = lax.broadcasted_iota(jnp.int32, (SLOT, HEAD), 0)
+    l_sub = lax.broadcasted_iota(jnp.int32, (MAIN, HEAD), 0)
     for turn, a in enumerate(ORDER):
         low = a * GROUP
 
@@ -272,21 +265,26 @@
         w = jnp.exp2((s - top) * FACTOR)
         o = dot(w.astype(BF16), prefix_values)
         total = o[:, HEAD:]
-        back[low:low + GROUP] = (o[:, :HEAD] / total).astype(BF16).reshape(GROUP, SLOT, HEAD)
+        back[low:low + GROUP, :SLOT] = (o[:, :HEAD] / total).astype(BF16).reshape(GROUP, SLOT, HEAD)
         lse = top * FACTOR + jnp.log2(total)
         for i in range(GROUP):
             piece_l = lse[i * SLOT:(i + 1) * SLOT]
-            lback[low + i] = jnp.sum(jnp.where(lane == sub, piece_l, 0.0), axis=0, keepdims=True)
+            l_row = jnp.sum(jnp.where(lane == sub, piece_l, 0.0), axis=0, keepdims=True)
+            l_high = l_row.astype(BF16).astype(F32)
+            l_mid = (l_row - l_high).astype(BF16).astype(F32)
+            l_low = l_row - l_high - l_mid
+            l_block = jnp.where(
+                l_sub == 0, l_high, jnp.where(l_sub == 1, l_mid, jnp.where(l_sub == 2, l_low, 0.0))
+            )
+            back[low + i, SLOT:] = l_block.astype(BF16)
 
         for d in range(max(low, 1), low + GROUP):
             give(d).start()
-            give_l(d).start()
         if turn == 0:
             for j, r, half in shares:
                 far(j, r, half).start()
 
     ret[0] = back[0]
-    lret[0] = lback[0]
 
     def hop(way, k, i):
         if way == 0:
@@ -306,8 +304,7 @@
 
     cols = lax.broadcasted_iota(jnp.int32, (rows_n, HOLDERS * MAIN), 1)
     from_main = one_hot(cols == jnp.where(place < MAIN, slot * MAIN + place, -1))
-    slots = lax.broadcasted_iota(jnp.int32, (rows_n, HOLDERS), 1)
-    from_slot = one_hot(slots == slot)
+    from_slot = one_hot((cols >= slot * MAIN) & (cols < slot * MAIN + 3))
     lanes = lax.broadcasted_iota(jnp.int32, (rows_n, HEAD), 1)
 
     for k in range(PER):
@@ -317,18 +314,12 @@
 
     for d in range(1, HOLDERS):
         give(d).wait_recv()
-        give_l(d).wait_recv()
     for j, r, half in shares:
         far(j, r, half).wait_recv()
     ring_start(0, 0)
 
-    l_all = lret[...].reshape(HOLDERS, HEAD)
-    l_high = l_all.astype(BF16)
-    l_rest = l_all - l_high.astype(F32)
-    l_mid = l_rest.astype(BF16)
-    l_low = (l_rest - l_mid.astype(F32)).astype(BF16)
-    l_rows = dot(from_slot, l_high) + dot(from_slot, l_mid) + dot(from_slot, l_low)
-    tails = ret[:, PER * MAIN:, :].reshape(HOLDERS * MAIN, HEAD)
+    l_rows = dot(from_slot, ret[:, SLOT:, :].reshape(HOLDERS * MAIN, HEAD))
+    tails = ret[:, PER * MAIN:SLOT, :].reshape(HOLDERS * MAIN, HEAD)
     for k in range(PER):
         mains = ret[:, k * MAIN:(k + 1) * MAIN, :].reshape(HOLDERS * MAIN, HEAD)
         pre = dot(from_main, mains) + dot(from_tail[k], tails)
@@ -383,7 +374,6 @@
             for d in range(1, HOLDERS):
                 dispatch(d).wait_send()
                 give(d).wait_send()
-                give_l(d).wait_send()
             give_own.wait_send()
             for j, r, half in shares:
                 far(j, r, half).wait_send()
@@ -441,7 +431,7 @@
     dma = sems((HOLDERS,))
     one = sems
     slots = pltpu.VMEM((HOLDERS, SLOT, HEAD), BF16)
-    lses = pltpu.VMEM((HOLDERS, 1, HEAD), F32)
+    results = pltpu.VMEM((HOLDERS, SLOT + MAIN, HEAD), BF16)
     return pl.pallas_call(
         attend_kernel,
         out_shape=pltpu.VMEM((rows_n, wide_out), BF16),
@@ -451,7 +441,7 @@
             pltpu.VMEM(queries.shape, BF16), pltpu.VMEM(suffix_kv.shape, BF16),
             pltpu.VMEM(cache.shape, BF16),
             pltpu.VMEM((PER, rows_n, HOLDERS * MAIN), BF16), sems((3,)),
-            slots, slots, slots, slots, lses, lses,
+            slots, slots, results, results,
             pltpu.VMEM((PER, rows_n, HEAD), F32),
             pltpu.VMEM((PER, rows_n, HEAD), F32),
             pltpu.VMEM((CORES, width, pair_out), BF16),
@@ -462,7 +452,7 @@
             pltpu.VMEM((2, rows_n, pair_out), F32),
             pltpu.VMEM((rows_n, pair_out), BF16),
             pltpu.VMEM((rows_n, pair_out), BF16),
-            dma, dma, dma, dma, dma, dma,
+            dma, dma, dma, dma,
             one, one, one,
             sems((RING - 1, CORES, HALVES)), sems((RING - 1, CORES, HALVES)),
             sems((HALVES, 2, 2, 2)), sems((HALVES, 2, 2, 2)),

time: 66.8 us -> 66.8 us (level)
  no operation moved by 1% of the time
where the time goes in v6:
time: 66.8 us; the launch traced here: 65.5 us
  Pallas kernels  64.7 us (97%)
  local copies, waits for them, and re-layouts  0.8 us (1%)
    pallas_call x1, Pallas kernels, attend(): pl.pallas_call(attend_kernel, out_shape=pltpu.VMEM((rows_n, wide_out), BF...  64.7 us

profile of v6, /device:TPU:1, one launch (start us, length us, event | category | flops | bytes accessed | tf_op | source)
XLA Modules:
  0.0 65.5 jit_solution(8054392804109376615)
XLA Ops:
  0.0 64.7 %attend.1 = bf16[256,1024]{1,0:T(8,128)(2,1)S(1)} custom-call(bf16[256,512]{1,0:T(8,128)(2,1)} %q_in.1, bf16[256,2,128]{2,1,0:T(2,128)(2,1)} %kv_in.1, bf16[1,2,1536,128]{3,2,1,0:T(8,128)(2,1)} %cache_in.1, bf16[512,8192]{1,0:T(8,128)(2,1)} %weight.1, s32[1,16]{1,0:T(1,128)} %readers.1, s32[32]{0:T(128)} %owner.1, s32[1,16]{1,0:T(1,128)} %lengths.1), custom_call_target="tpu_custom_call" | custom-call | flops 2013265920 | bytes 4194304 | tf_op jit(solution)/shard_map/attend/pallas_call | solution.py:435
  64.7 0.8 %copy.9 = bf16[256,1024]{1,0:T(8,128)(2,1)} copy(bf16[256,1024]{1,0:T(8,128)(2,1)S(1)} %attend.1) | data formatting | bytes 1048576
